TPU v7x, 32 devices: a whole 2x2x4 slice. The times are simulated.
32 devices in a mesh: group: 4 (over y, core), member: 8 (over z, x).
Axes of the slice: x: 2, y: 2, z: 4, core: 2. Of those that a mesh axis runs over, the one named last changes fastest.
Arguments:
- candidates: bfloat16 [512, 32, 1024], P('member', 'group'), may hold values from -6 to 6
- kv_cache: bfloat16 [32, 2048, 2048], P('group', 'member'), may hold values from -6 to 6
- cache_request: int32 [32], replicated, may hold values from 0 to 31, as said below
- rank_request: int32 [32], replicated, may hold values from 0 to 31, as said below
- hist_blocks: int32 [32], replicated, may hold values from 1 to 16, 272 in all
- w_uq: bfloat16 [1024, 2048], replicated, may hold values from -0.1875 to 0.1875
- w_out: bfloat16 [1024, 1024], replicated, may hold values from -0.1875 to 0.1875
Outputs:
- ranked: bfloat16 [512, 32, 1024], P('member', 'group')
Inputs may be any that keep to these rules, and one draw needn't show every extreme that they name: `cache_request`: A permutation; cache row q lies on group q // 8, events split over member. `rank_request`: A permutation; group g ranks positions g * 8 to (g + 1) * 8 - 1. The requests cached on one group are dealt out to the ranking groups in turn, so every pair of groups carries 8 // 4 or 2 requests and some pair carries exactly 2; the uneven part of the load is the live history lengths.
All inputs are finite; a program needn't handle non-finite values.
Results may differ from a plain program's by a relative error of at most 0.011.
Values may be sent and summed in bfloat16 or wider, within the bound.
A program may use at most 320 MiB of HBM per device.

v0:
```python
import jax
import jax.numpy as jnp
from jax import lax
from jax.sharding import PartitionSpec as P

HEADS = 8
BLK = 128


def layer_norm(values):
    center = values - jnp.mean(values, axis=-1, keepdims=True)
    spread = jnp.mean(center * center, axis=-1, keepdims=True)
    return center * lax.rsqrt(spread + 1e-05)


def routing(cache_request, rank_request, per_group):
    slot_ids = jnp.arange(cache_request.shape[0], dtype=jnp.int32)
    match = cache_request[:, None] == rank_request[None, :]
    rank_pos = jnp.sum(jnp.where(match, slot_ids[None, :], 0), axis=1)
    target = rank_pos // per_group
    owner_grp = slot_ids // per_group
    earlier = (
        (owner_grp[:, None] == owner_grp[None, :])
        & (target[:, None] == target[None, :])
        & (slot_ids[None, :] < slot_ids[:, None])
    )
    arrival = jnp.sum(earlier.astype(jnp.int32), axis=1)
    slot_of_pos = jnp.sum(jnp.where(match, slot_ids[:, None], 0), axis=0)
    return (target, arrival, slot_of_pos)


def attend(piece, queries, live, scale):
    width = queries.shape[2] * queries.shape[3]
    count = piece.shape[1]
    keys = piece[:, :, :width].reshape(piece.shape[0], count, queries.shape[2], queries.shape[3])
    values = piece[:, :, width:].reshape(piece.shape[0], count, queries.shape[2], queries.shape[3])
    scores = jnp.einsum("crhd,rehd->rhce", queries, keys, preferred_element_type=jnp.float32)
    events = jnp.arange(count).astype(jnp.float32)
    keep = (events[None, :] < live[:, None]).astype(jnp.float32) / live[:, None]
    weights = (jax.nn.silu(scores * scale) * keep[:, None, None, :]).astype(jnp.bfloat16)
    return jnp.einsum("rhce,rehd->crhd", weights, values, preferred_element_type=jnp.float32)


def on_device(candidates, kv_cache, cache_request, rank_request, hist_blocks, w_uq, w_out):
    groups = lax.axis_size("group")
    per_group = kv_cache.shape[0]
    cand_rows = candidates.shape[0]
    width = candidates.shape[2]
    head_dim = width // HEADS
    capacity = (per_group + groups - 1) // groups
    group_now = lax.axis_index("group")
    target, arrival, slot_of_pos = routing(cache_request, rank_request, per_group)
    first_slot = group_now * per_group
    local_target = lax.dynamic_slice_in_dim(target, first_slot, per_group)
    local_arrival = lax.dynamic_slice_in_dim(arrival, first_slot, per_group)
    target_grid = jnp.arange(groups)[:, None, None]
    place_grid = jnp.arange(capacity)[None, :, None]
    hits = (local_target[None, None, :] == target_grid) & (
        local_arrival[None, None, :] == place_grid
    )
    chosen = jnp.sum(jnp.where(hits, jnp.arange(per_group)[None, None, :], 0), axis=2).reshape(-1)
    filled = jnp.any(hits, axis=2).reshape(-1)
    positions = first_slot + jnp.arange(per_group)
    source_slot = slot_of_pos[positions]
    receive_index = source_slot // per_group * capacity + arrival[source_slot]
    live = (hist_blocks[rank_request[positions]] * BLK).astype(jnp.float32)
    inputs = candidates.astype(jnp.float32)
    normed = layer_norm(inputs).astype(jnp.bfloat16).reshape(cand_rows * per_group, width)
    projected = jax.nn.silu(jnp.dot(normed, w_uq, preferred_element_type=jnp.float32))
    gates = projected[:, :width].reshape(cand_rows, per_group, width)
    queries = (
        projected[:, width:].astype(jnp.bfloat16).reshape(cand_rows, per_group, HEADS, head_dim)
    )
    scale = head_dim ** (-0.5)
    outgoing = jnp.where(filled[:, None, None], kv_cache[chosen], jnp.zeros((), jnp.bfloat16))
    incoming = lax.all_to_all(outgoing, "group", split_axis=0, concat_axis=0, tiled=True)
    panels = incoming[receive_index]
    attn = attend(lax.all_gather(panels, "member", axis=1, tiled=True), queries, live, scale)
    attn = attn.reshape(cand_rows, per_group, width)
    gated = (layer_norm(attn) * gates).astype(jnp.bfloat16).reshape(cand_rows * per_group, width)
    result = jnp.dot(gated, w_out, preferred_element_type=jnp.float32) + inputs.reshape(
        cand_rows * per_group, width
    )
    return result.astype(jnp.bfloat16).reshape(cand_rows, per_group, width)


def solution(mesh):
    return jax.shard_map(
        on_device,
        mesh=mesh,
        in_specs=(P("member", "group", None), P("group", "member", None), P(), P(), P(), P(), P()),
        out_specs=P("member", "group", None),
        check_vma=False,
    )
```

profile of v0, /device:TPU:25, one launch (start us, length us, event | category | flops | bytes accessed | tf_op | source)
XLA Modules:
  0.0 1574.5 jit_solution(17651629855079412787)
XLA Ops:
  6.5 1.0 fusion.25
  7.6 0.2 convert_reduce_fusion.1
  7.9 0.1 fusion.27
  8.1 0.2 and_reduce_fusion
  8.2 0.1 copy.59
  8.4 0.1 copy.58
  8.5 0.1 broadcast_in_dim.47
  8.6 8.0 gather_fusion
  16.7 7.2 broadcast_select_fusion
  23.9 6.3 all-to-all-start
  30.2 0.6 gather_fusion.1
  30.8 0.6 gather_fusion.2
  31.5 91.0 %all-to-all-done = bf16[8,256,2048]{2,1,0:T(8,128)(2,1)} async-done(((bf16[8,256,2048]{2,1,0:T(8,128)(2,1)}), bf16[8,256,2048]{2,1,0:T(8,128)(2,1)}, u32[]{:S(2)}, u32[]{:S(2)}) %all-to-all-start) | async-done | bytes 8388640 | tf_op jit(solution)/shard_map/all_to_all | solution.py:76
  122.5 8.0 gather_fusion.3
  130.6 0.6 copy-done.1
  131.2 0.6 gather_fusion.4
  131.8 0.2 convert_reduce_fusion
  132.1 0.1 copy.62
  132.2 0.4 fusion.3
  132.8 0.6 gather_fusion.5
  133.5 5.1 divide_multiply_fusion
  138.5 1.9 copy-done.4
  140.5 1.2 fusion.11
  141.7 1256.3 %all-gather.3.cloned.1.call-done = bf16[8,2048,2048]{2,1,0:T(8,128)(2,1)} async-done(((bf16[8,256,2048]{2,1,0:T(8,128)(2,1)}), bf16[8,2048,2048]{2,1,0:T(8,128)(2,1)}) %all-gather.3.cloned.1.call-update) | async-done | bytes 67108880 | tf_op jit(solution)/shard_map/all_gather | solution.py:78
  1398.0 43.3 %fusion.35 = (bf16[8,2048,1024]{2,1,0:T(8,128)(2,1)}, bf16[8,2048,1024]{2,1,0:T(8,128)(2,1)}) fusion(bf16[8,2048,2048]{2,1,0:T(8,128)(2,1)} %all-gather.3.cloned.1.call-done), kind=kLoop, calls=%fused_computation.85 | loop fusion | bytes 134217728 | tf_op jit(solution)/shard_map/slice | solution.py:35
  1441.3 42.2 %copy.60 = bf16[8,2048,1024]{1,2,0:T(8,128)(2,1)} copy(bf16[8,2048,1024]{2,1,0:T(8,128)(2,1)} %get-tuple-element.8) | data formatting | bytes 67108864 | tf_op jit(solution)/shard_map/slice | solution.py:36
  1483.6 42.2 %copy.65 = bf16[8,2048,1024]{1,2,0:T(8,128)(2,1)} copy(bf16[8,2048,1024]{2,1,0:T(8,128)(2,1)} %get-tuple-element.7) | data formatting | bytes 67108864 | tf_op jit(solution)/shard_map/slice | solution.py:35
  1525.8 34.1 %fusion.36 = (f32[64,8]{0,1:T(8,128)S(1)}, f32[64,8,8,128]{3,0,2,1:T(8,128)}) fusion(bf16[8,2048,8,128]{1,3,2,0:T(8,128)(2,1)} %bitcast.59, bf16[8,2048,8,128]{1,3,2,0:T(8,128)(2,1)} %bitcast.60, f32[8,2048]{1,0:T(8,128)S(1)} %convert_divide_fusion, bf16[64,8,8,128]{3,1,2,0:T(8,128)(2,1)} %fusion.11), kind=kOutput, calls=%fused_computation.86 | convolution fusion | flops 4354211328 | bytes 70322176 | tf_op jit(solution)/shard_map/rhce,rehd->crhd/dot_general | solution.py:41
  1560.1 1.9 multiply_reduce_fusion
  1562.1 0.1 rsqrt.21
  1562.2 0.1 div.75
  1562.3 5.3 fusion.10
  (38 shorter events, 0.9 us)
Async XLA Ops:
  6.5 1555.8 %copy-start = (bf16[1024,1024]{1,0:T(8,128)(2,1)S(1)}, bf16[1024,1024]{1,0:T(8,128)(2,1)}, u32[]{:S(2)}) copy-start(bf16[1024,1024]{1,0:T(8,128)(2,1)} %param.13) | copy-start | bytes 6291460
  23.9 98.6 %all-to-all-start = ((bf16[8,256,2048]{2,1,0:T(8,128)(2,1)}), bf16[8,256,2048]{2,1,0:T(8,128)(2,1)}, u32[]{:S(2)}, u32[]{:S(2)}) async-start(bf16[8,256,2048]{2,1,0:T(8,128)(2,1)} %broadcast_select_fusion), calls=%async_computation | async-start | bytes 16777216 | tf_op jit(solution)/shard_map/all_to_all | solution.py:76
  30.2 1367.9 %all-gather.3.cloned.1.call-start = ((), (), s32[]{:S(2)}) async-start(), calls=%async_computation.1 | async-start | bytes 75497472 | tf_op jit(solution)/shard_map/all_gather | solution.py:78
  130.5 0.7 copy-start.1
  130.5 1.3 copy-start.3
  130.5 2.3 copy-start.2
  138.5 1.9 copy-start.4
Sparse Core Ops, SparseCore 0:
  130.7 1267.3 all-gather.2
where the time goes:
time: 1580 us; the launch traced here: 1570 us
  waiting for transfers between devices  1350 us (85%)
  local copies, waits for them, and re-layouts  151 us (10%)
  matrix products  44.6 us (3%)
    all_gather x1, waiting for transfers between devices, on_device(): lax.all_gather(panels, 'member', axis=1, tiled=True)  1260 us
    all_to_all x1, waiting for transfers between devices, on_device(): lax.all_to_all(outgoing, 'group', split_axis=0, concat_axis=0, tiled=True)  91 us
    slice x2, local copies, waits for them, and re-layouts, attend(): piece[:, :, :width]  85.6 us
    slice x1, local copies, waits for them, and re-layouts, attend(): piece[:, :, width:]  42.2 us
    dot_general x1, matrix products, attend(): jnp.einsum('rhce,rehd->crhd', weights, values, preferred_element_type=jnp...  34.1 us
  transfers between devices with their start and end apart: 2, of which 2 were waited for; matrix products, arithmetic and copies ran while one was open for 1% of the time, Pallas kernels for 0%

commit v1 on v0

v1 whole, which is shorter than its diff:
```python
import jax
import jax.numpy as jnp
from jax import lax
from jax.sharding import PartitionSpec as P

HEADS = 8
BLK = 128


def layer_norm(values):
    center = values - jnp.mean(values, axis=-1, keepdims=True)
    spread = jnp.mean(center * center, axis=-1, keepdims=True)
    return center * lax.rsqrt(spread + 1e-05)


def routing(cache_request, rank_request, per_group):
    slot_ids = jnp.arange(cache_request.shape[0], dtype=jnp.int32)
    match = cache_request[:, None] == rank_request[None, :]
    rank_pos = jnp.sum(jnp.where(match, slot_ids[None, :], 0), axis=1)
    target = rank_pos // per_group
    owner_grp = slot_ids // per_group
    earlier = (
        (owner_grp[:, None] == owner_grp[None, :])
        & (target[:, None] == target[None, :])
        & (slot_ids[None, :] < slot_ids[:, None])
    )
    arrival = jnp.sum(earlier.astype(jnp.int32), axis=1)
    slot_of_pos = jnp.sum(jnp.where(match, slot_ids[:, None], 0), axis=0)
    return (target, arrival, slot_of_pos)


def inverse(order):
    ids = jnp.arange(order.shape[0], dtype=jnp.int32)
    return jnp.sum(jnp.where(order[None, :] == ids[:, None], ids[None, :], 0), axis=1)


def on_device(candidates, kv_cache, cache_request, rank_request, hist_blocks, w_uq, w_out):
    groups = lax.axis_size("group")
    per_group, count, _ = kv_cache.shape
    cand_rows = candidates.shape[0]
    width = candidates.shape[2]
    head_dim = width // HEADS
    cap = per_group // groups
    group_now = lax.axis_index("group")
    member_now = lax.axis_index("member")
    target, arrival, slot_of_pos = routing(cache_request, rank_request, per_group)
    first = group_now * per_group
    local = first + jnp.arange(per_group, dtype=jnp.int32)
    source = slot_of_pos[local]
    unit_of_pos = source // per_group * cap + arrival[source]
    pos_of_unit = inverse(unit_of_pos)
    unit_of_slot = target[local] * cap + arrival[local]
    slot_of_unit = inverse(unit_of_slot)
    live = hist_blocks[cache_request[local]] * BLK

    inputs = candidates.astype(jnp.float32)
    normed = layer_norm(inputs).astype(jnp.bfloat16).reshape(cand_rows * per_group, width)
    projected = jax.nn.silu(jnp.dot(normed, w_uq, preferred_element_type=jnp.float32))
    gates = projected[:, :width].reshape(cand_rows, per_group, width)
    queries = projected[:, width:].astype(jnp.bfloat16).reshape(cand_rows, per_group, width)
    outgoing = jnp.transpose(queries, (1, 0, 2))[pos_of_unit]
    incoming = lax.all_to_all(outgoing, "group", split_axis=0, concat_axis=0, tiled=True)
    incoming = incoming[unit_of_slot]
    every = lax.all_gather(incoming, "member", axis=1, tiled=True)
    every = every.reshape(per_group, every.shape[1], HEADS, head_dim)
    keys = kv_cache[:, :, :width].reshape(per_group, count, HEADS, head_dim)
    values = kv_cache[:, :, width:].reshape(per_group, count, HEADS, head_dim)
    half = jnp.einsum("rchd,rehd->rhce", every, keys, preferred_element_type=jnp.float32) * (
        0.5 * head_dim**-0.5
    )
    events = member_now * count + jnp.arange(count)
    keep = (events[None, :] < live[:, None]).astype(jnp.float32) / live[:, None]
    weights = ((half + half * jnp.tanh(half)) * keep[:, None, None, :]).astype(jnp.bfloat16)
    partial = jnp.einsum("rhce,rehd->rchd", weights, values, preferred_element_type=jnp.float32)
    partial = partial.astype(jnp.bfloat16).reshape(per_group, every.shape[1], width)
    summed = lax.psum_scatter(partial, "member", scatter_dimension=1, tiled=True)
    back = lax.all_to_all(summed[slot_of_unit], "group", split_axis=0, concat_axis=0, tiled=True)
    attn = jnp.transpose(back[unit_of_pos], (1, 0, 2)).astype(jnp.float32)
    gated = (layer_norm(attn) * gates).astype(jnp.bfloat16).reshape(cand_rows * per_group, width)
    result = jnp.dot(gated, w_out, preferred_element_type=jnp.float32) + inputs.reshape(
        cand_rows * per_group, width
    )
    return result.astype(jnp.bfloat16).reshape(cand_rows, per_group, width)


def solution(mesh):
    return jax.shard_map(
        on_device,
        mesh=mesh,
        in_specs=(P("member", "group", None), P("group", "member", None), P(), P(), P(), P(), P()),
        out_specs=P("member", "group", None),
        check_vma=False,
    )
```

time: 1580 us -> 395 us (0.25)
  waiting for transfers between devices: 1350 us -> 273 us
  local copies, waits for them, and re-layouts: 151 us -> 58.9 us
  matrix products: 44.6 us -> 27 us
    all_gather x1, waiting for transfers between devices: 1260 us -> 103 us  [on_device(): every = lax.all_gather(incoming, 'member', axis=1, tiled=True)]
    reduce_scatter x0 -> x1, waiting for transfers between devices: none -> 147 us  [on_device(): lax.psum_scatter(partial, 'member', scatter_dimension=1, tiled=True)]
    slice x3 -> x2, local copies, waits for them, and re-layouts: 128 us -> 12.4 us  [the longest x1 6.49 us: on_device(): values = kv_cache[:, :, width:].reshape(per_group, count, HEADS, head_dim)]
    all_to_all x1, waiting for transfers between devices: 91 us -> 12.3 us  [on_device(): lax.all_to_all(outgoing, 'group', split_axis=0, concat_axis=0, tiled=True)]
  transfers between devices with their start and end apart: 2 -> 4, of which waited for: 2 -> 4; matrix products, arithmetic and copies ran while one was open for 1% -> 6% of each run, Pallas kernels for 0% -> 0%
where the time goes in v1:
time: 395 us; the launch traced here: 390 us
  waiting for transfers between devices  273 us (69%)
  local copies, waits for them, and re-layouts  58.9 us (15%)
  matrix products  27 us (7%)
  between operations  13.6 us (3%)
  starting transfers between devices  8.82 us (2%)
  other arithmetic  8.18 us (2%)
    reduce_scatter x1, waiting for transfers between devices, on_device(): lax.psum_scatter(partial, 'member', scatter_dimension=1, tiled=True)  147 us
    all_gather x1, waiting for transfers between devices, on_device(): every = lax.all_gather(incoming, 'member', axis=1, tiled=True)  103 us
    dot_general x1, matrix products, on_device(): jnp.einsum('rhce,rehd->rchd', weights, values, preferred_element_type=jnp...  19.2 us
    all_to_all x1, waiting for transfers between devices, on_device(): lax.all_to_all(outgoing, 'group', split_axis=0, concat_axis=0, tiled=True)  12.3 us
    reshape x1, local copies, waits for them, and re-layouts, on_device(): partial.astype(jnp.bfloat16).reshape(per_group, every.shape[1], width)  11.4 us
    all_gather x1, local copies, waits for them, and re-layouts, on_device(): every = lax.all_gather(incoming, 'member', axis=1, tiled=True)  11.4 us
    all_to_all x1, waiting for transfers between devices, on_device(): lax.all_to_all(summed[slot_of_unit], 'group', split_axis=0, concat_axis=0...  10.5 us
  transfers between devices with their start and end apart: 4, of which 4 were waited for; matrix products, arithmetic and copies ran while one was open for 6% of the time, Pallas kernels for 0%

profile of v1, /device:TPU:25, one launch (start us, length us, event | category | flops | bytes accessed | tf_op | source)
XLA Modules:
  0.0 389.7 jit_solution(12948929465501244490)
XLA Ops:
  6.5 1.0 fusion.33
  7.6 0.6 gather_fusion
  8.4 0.6 gather_fusion.1
  9.2 1.4 convert_reduce_fusion
  10.8 1.6 fusion.13
  12.6 5.4 %divide_multiply_fusion = f32[512,2048]{1,0:T(8,128)S(1)} fusion(bf16[1024,2048]{1,0:T(8,128)(2,1)} %param.12, bf16[64,8,1024]{2,1,0:T(8,128)(2,1)} %param.7, f32[64,8]{1,0:T(8,128)S(1)} %copy.67, f32[64,8]{1,0:T(8,128)S(1)} %copy.65), kind=kOutput, calls=%fused_computation.18 | convolution fusion | flops 2153775104 | bytes 9441280 | tf_op jit(solution)/shard_map/dot_general | solution.py:58
  18.2 0.6 copy.86
  18.8 1.2 copy-done.4
  19.9 1.6 gather_fusion.2
  21.5 4.2 %all-to-all-start = ((bf16[8,64,1024]{2,1,0:T(8,128)(2,1)}), bf16[8,64,1024]{2,1,0:T(8,128)(2,1)S(1)}, u32[]{:S(2)}, u32[]{:S(2)}) async-start(bf16[8,64,1024]{2,1,0:T(8,128)(2,1)} %gather_fusion.2), calls=%async_computation | async-start | bytes 2097152 | tf_op jit(solution)/shard_map/all_to_all | solution.py:62
  25.7 0.6 gather_fusion.3
  26.3 0.6 gather_fusion.4
  27.0 12.3 %all-to-all-done = bf16[8,64,1024]{2,1,0:T(8,128)(2,1)S(1)} async-done(((bf16[8,64,1024]{2,1,0:T(8,128)(2,1)}), bf16[8,64,1024]{2,1,0:T(8,128)(2,1)S(1)}, u32[]{:S(2)}, u32[]{:S(2)}) %all-to-all-start) | async-done | bytes 1048608 | tf_op jit(solution)/shard_map/all_to_all | solution.py:62
  39.3 1.6 gather_fusion.5
  40.9 0.6 gather_fusion.6
  41.6 5.9 %fusion.45 = (bf16[8,256,1024]{2,1,0:T(8,128)(2,1)}, bf16[8,256,1024]{2,1,0:T(8,128)(2,1)}) fusion(bf16[8,256,2048]{2,1,0:T(8,128)(2,1)} %param.8), kind=kLoop, calls=%fused_computation.107 | loop fusion | bytes 16777216 | tf_op jit(solution)/shard_map/slice | solution.py:66
  47.5 6.6 %copy.79 = bf16[8,256,1024]{1,2,0:T(8,128)(2,1)} copy(bf16[8,256,1024]{2,1,0:T(8,128)(2,1)} %get-tuple-element.9) | data formatting | bytes 8388608
  54.1 6.5 %copy.73 = bf16[8,256,1024]{1,2,0:T(8,128)(2,1)} copy(bf16[8,256,1024]{2,1,0:T(8,128)(2,1)} %get-tuple-element.10) | data formatting | bytes 8388608 | tf_op jit(solution)/shard_map/slice | solution.py:67
  60.6 0.6 gather_fusion.7
  61.3 103.1 %all-gather.3.cloned.1.call-done = bf16[8,512,1024]{2,1,0:T(8,128)(2,1)} async-done(((bf16[8,64,1024]{2,1,0:T(8,128)(2,1)}), bf16[8,512,1024]{2,1,0:T(8,128)(2,1)}) %all-gather.3.cloned.1.call-update) | async-done | bytes 8388624 | tf_op jit(solution)/shard_map/all_gather | solution.py:64
  164.5 11.4 %copy.69 = bf16[8,512,1024]{1,2,0:T(8,128)(2,1)} copy(bf16[8,512,1024]{2,1,0:T(8,128)(2,1)} %all-gather.3.cloned.1.call-done) | data formatting | bytes 16777216 | tf_op jit(solution)/shard_map/all_gather | solution.py:64
  175.9 19.2 %fusion.8 = bf16[8,8,512,128]{2,3,1,0:T(8,128)(2,1)} fusion(bf16[8,256,8,128]{1,3,2,0:T(8,128)(2,1)} %bitcast.90, f32[8,256]{1,0:T(8,128)S(1)} %convert_divide_fusion, bf16[8,512,8,128]{1,3,2,0:T(8,128)(2,1)} %bitcast.86, bf16[8,256,8,128]{1,3,2,0:T(8,128)(2,1)} %bitcast.89), kind=kOutput, calls=%fused_computation.17 | convolution fusion | flops 4341104640 | bytes 25174016 | tf_op jit(solution)/shard_map/rhce,rehd->rchd/dot_general | solution.py:74
  195.1 11.4 %copy.74 = bf16[8,512,1024]{2,1,0:T(8,128)(2,1)} copy(bf16[8,512,1024]{1,2,0:T(8,128)(2,1)} %bitcast.87) | data formatting | bytes 16777216 | tf_op jit(solution)/shard_map/reshape | solution.py:75
  206.7 147.3 %reduce-scatter.2.cloned.1.call-done = bf16[8,64,1024]{2,1,0:T(8,128)(2,1)} async-done(((bf16[8,512,1024]{2,1,0:T(8,128)(2,1)}), bf16[8,64,1024]{2,1,0:T(8,128)(2,1)}) %reduce-scatter.2.cloned.1.call-update) | async-done | bytes 1048592 | tf_op jit(solution)/shard_map/reduce_scatter | solution.py:76
  354.0 2.8 gather_fusion.8
  356.8 4.6 %all-to-all-start.1 = ((bf16[8,64,1024]{2,1,0:T(8,128)(2,1)}), bf16[8,64,1024]{2,1,0:T(8,128)(2,1)}, u32[]{:S(2)}, u32[]{:S(2)}) async-start(bf16[8,64,1024]{2,1,0:T(8,128)(2,1)} %gather_fusion.8), calls=%async_computation.2 | async-start | bytes 2097152 | tf_op jit(solution)/shard_map/all_to_all | solution.py:77
  361.4 3.2 slice_bitcast_fusion
  364.6 10.5 %all-to-all-done.1 = bf16[8,64,1024]{2,1,0:T(8,128)(2,1)} async-done(((bf16[8,64,1024]{2,1,0:T(8,128)(2,1)}), bf16[8,64,1024]{2,1,0:T(8,128)(2,1)}, u32[]{:S(2)}, u32[]{:S(2)}) %all-to-all-start.1) | async-done | bytes 1048608 | tf_op jit(solution)/shard_map/all_to_all | solution.py:77
  375.1 1.8 gather_fusion.9
  377.2 0.4 fusion.19
  377.6 2.8 fusion.21
  380.5 2.4 fusion.22
  (45 shorter events, 1.4 us)
Async XLA Ops:
  6.5 373.9 %copy-start = (bf16[1024,1024]{1,0:T(8,128)(2,1)S(1)}, bf16[1024,1024]{1,0:T(8,128)(2,1)}, u32[]{:S(2)}) copy-start(bf16[1024,1024]{1,0:T(8,128)(2,1)} %param.13) | copy-start | bytes 6291460
  18.0 1.9 copy-start.4
  19.9 21.0 %copy-start.1 = (s32[32]{0:T(128)S(1)}, s32[32]{0:T(128)}, u32[]{:S(2)}) copy-start(s32[32]{0:T(128)} %param.9) | copy-start | bytes 388
  21.5 17.8 %all-to-all-start = ((bf16[8,64,1024]{2,1,0:T(8,128)(2,1)}), bf16[8,64,1024]{2,1,0:T(8,128)(2,1)S(1)}, u32[]{:S(2)}, u32[]{:S(2)}) async-start(bf16[8,64,1024]{2,1,0:T(8,128)(2,1)} %gather_fusion.2), calls=%async_computation | async-start | bytes 2097152 | tf_op jit(solution)/shard_map/all_to_all | solution.py:62
  25.7 138.8 %all-gather.3.cloned.1.call-start = ((), (), s32[]{:S(2)}) async-start(), calls=%async_computation.4 | async-start | bytes 9437184 | tf_op jit(solution)/shard_map/all_gather | solution.py:64
  40.9 313.1 %reduce-scatter.2.cloned.1.call-start = ((), (), s32[]{:S(2)}) async-start(), calls=%async_computation.3 | async-start | bytes 9437184 | tf_op jit(solution)/shard_map/reduce_scatter | solution.py:76
  54.1 6.5 %copy-start.2 = (s32[32]{0:T(128)S(1)}, s32[32]{0:T(128)}, u32[]{:S(2)}) copy-start(s32[32]{0:T(128)} %param.11) | copy-start | bytes 388
  356.8 18.3 %all-to-all-start.1 = ((bf16[8,64,1024]{2,1,0:T(8,128)(2,1)}), bf16[8,64,1024]{2,1,0:T(8,128)(2,1)}, u32[]{:S(2)}, u32[]{:S(2)}) async-start(bf16[8,64,1024]{2,1,0:T(8,128)(2,1)} %gather_fusion.8), calls=%async_computation.2 | async-start | bytes 2097152 | tf_op jit(solution)/shard_map/all_to_all | solution.py:77
  377.0 3.5 copy-start.3
Sparse Core Ops, SparseCore 0:
  41.0 123.4 all-gather.2
  206.7 147.2 reduce-scatter.1

commit v2 on v1

v2 whole, which is shorter than its diff:
```python
import functools

import jax
import jax.numpy as jnp
from jax import lax
from jax.experimental import pallas as pl
from jax.experimental.pallas import tpu as pltpu
from jax.sharding import PartitionSpec as P

HEADS = 8
BLK = 128
LINE = 4


def layer_norm(values):
    center = values - jnp.mean(values, axis=-1, keepdims=True)
    spread = jnp.mean(center * center, axis=-1, keepdims=True)
    return center * lax.rsqrt(spread + 1e-05)


def routing(cache_request, rank_request, per_group):
    slot_ids = jnp.arange(cache_request.shape[0], dtype=jnp.int32)
    match = cache_request[:, None] == rank_request[None, :]
    rank_pos = jnp.sum(jnp.where(match, slot_ids[None, :], 0), axis=1)
    target = rank_pos // per_group
    owner_grp = slot_ids // per_group
    earlier = (
        (owner_grp[:, None] == owner_grp[None, :])
        & (target[:, None] == target[None, :])
        & (slot_ids[None, :] < slot_ids[:, None])
    )
    arrival = jnp.sum(earlier.astype(jnp.int32), axis=1)
    slot_of_pos = jnp.sum(jnp.where(match, slot_ids[:, None], 0), axis=0)
    return (target, arrival, slot_of_pos)


def inverse(order):
    ids = jnp.arange(order.shape[0], dtype=jnp.int32)
    return jnp.sum(jnp.where(order[None, :] == ids[:, None], ids[None, :], 0), axis=1)


def kernel(
    dims,
    slot_ref,
    live_ref,
    share_ref,
    q_ref,
    kv_hbm,
    out_ref,
    kv,
    qbuf,
    pbuf,
    prec,
    ssum,
    fin,
    kv_sem,
    s1,
    r1,
    s2,
    r2,
    s3,
    r3,
    s4,
    r4,
):
    groups, lines, rows, cap = dims
    units = groups * cap
    cands, width = q_ref.shape[1:]
    count = kv_hbm.shape[1]
    head_dim = width // HEADS
    g = lax.axis_index("group")
    member = lax.axis_index("member")
    z = member // rows
    x = lax.rem(member, rows)

    def at(group, line, row):
        return {"group": group, "member": line * rows + row}

    def add(value, step, size):
        return lax.rem(value + step, size)

    panel = pltpu.make_async_copy(kv_hbm, kv, kv_sem)
    panel.start()
    barrier = pltpu.get_barrier_semaphore()
    peers = [(t, dz, 0) for t in range(groups) for dz in range(lines) if t or dz]
    peers += [(0, 0, dx) for dx in range(1, rows)]
    for t, dz, dx in peers:
        pl.semaphore_signal(
            barrier,
            inc=1,
            device_id=at(add(g, t, groups), add(z, dz, lines), add(x, dx, rows)),
            device_id_type=pl.DeviceIdType.MESH,
        )
    pl.semaphore_wait(barrier, len(peers))

    def ready(ref, sem):
        pltpu.make_async_copy(ref, ref, sem).wait()

    def remote(src, dst, send, recv, device):
        return pltpu.make_async_remote_copy(
            src_ref=src,
            dst_ref=dst,
            send_sem=send,
            recv_sem=recv,
            device_id=device,
            device_id_type=pl.DeviceIdType.MESH,
        )

    def scatter_queries(u, carry):
        t = u // cap
        for dz in range(lines):
            there = (add(g, t, groups), add(z, dz, lines), x)
            send = lambda: remote(
                q_ref.at[u], qbuf.at[u, x, z], s1.at[u, dz], r1.at[u, dz], at(*there)
            ).start()
            if dz:
                send()
            else:
                pl.when(t > 0)(send)
                pl.when(t == 0)(
                    lambda: pltpu.make_async_copy(
                        q_ref.at[u], qbuf.at[u, x, z], r1.at[u, 0]
                    ).start()
                )
        return carry

    lax.fori_loop(0, units, scatter_queries, 0)
    panel.wait()

    def forward(u):
        for dz in range(lines):
            ready(qbuf.at[u, x, add(z, lines - dz, lines)], r1.at[u, dz])
        for dx in range(1, rows):
            remote(
                qbuf.at[u, x],
                qbuf.at[u, x],
                s2.at[u, dx],
                r2.at[u, dx],
                at(g, z, add(x, dx, rows)),
            ).start()

    def attend(u):
        for dx in range(1, rows):
            ready(qbuf.at[u, add(x, rows - dx, rows)], r2.at[u, dx])
        slot = slot_ref[u]
        limit = live_ref[u] - member * count
        share = share_ref[u]
        keep = lax.broadcasted_iota(jnp.int32, (count, head_dim), 0) < limit
        keep = keep.astype(jnp.float32)
        for h in range(HEADS):
            cols = slice(h * head_dim, (h + 1) * head_dim)
            vals = slice(width + h * head_dim, width + (h + 1) * head_dim)
            q = qbuf[u, :, :, :, cols].reshape(rows * lines * cands, head_dim)
            k = kv[slot, :, cols]
            v = (kv[slot, :, vals].astype(jnp.float32) * keep).astype(jnp.bfloat16)
            score = lax.dot_general(
                q, k, (((1,), (1,)), ((), ())), preferred_element_type=jnp.float32
            )
            half = score * (0.5 * head_dim**-0.5)
            weight = (half + half * jnp.tanh(half)).astype(jnp.bfloat16)
            part = jnp.dot(weight, v, preferred_element_type=jnp.float32) * share
            pbuf[u, :, :, :, cols] = part.astype(jnp.bfloat16).reshape(
                rows, lines, cands, head_dim
            )
        for dx in range(1, rows):
            row = add(x, dx, rows)
            remote(
                pbuf.at[u, row], prec.at[u, dx], s3.at[u, dx], r3.at[u, dx], at(g, z, row)
            ).start()

    def give_back(u):
        t = u // cap
        for dx in range(1, rows):
            ready(prec.at[u, dx], r3.at[u, dx])
        total = pbuf[u, x].astype(jnp.float32)
        for dx in range(1, rows):
            total = total + prec[u, dx].astype(jnp.float32)
        ssum[u] = total.astype(jnp.bfloat16)
        for dz in range(lines):
            line = add(z, dz, lines)
            there = (add(g, groups - t, groups), line, x)
            send = lambda: remote(
                ssum.at[u, line], fin.at[u, dz], s4.at[u, dz], r4.at[u, dz], at(*there)
            ).start()
            if dz:
                send()
            else:
                pl.when(t > 0)(send)
                pl.when(t == 0)(
                    lambda: pltpu.make_async_copy(
                        ssum.at[u, line], fin.at[u, 0], r4.at[u, 0]
                    ).start()
                )

    def stage(i, carry):
        pl.when(i < units)(lambda: forward(i))
        pl.when((i >= 1) & (i < units + 1))(lambda: attend(i - 1))
        pl.when(i >= 2)(lambda: give_back(i - 2))
        return carry

    lax.fori_loop(0, units + 2, stage, 0)

    def collect(u, carry):
        for dz in range(lines):
            ready(fin.at[u, dz], r4.at[u, dz])
        total = fin[u, 0].astype(jnp.float32)
        for dz in range(1, lines):
            total = total + fin[u, dz].astype(jnp.float32)
        out_ref[u] = total
        return carry

    lax.fori_loop(0, units, collect, 0)

    def drain(u, carry):
        t = u // cap
        for dz in range(lines):
            def both():
                ready(q_ref.at[u], s1.at[u, dz])
                ready(ssum.at[u, add(z, dz, lines)], s4.at[u, dz])

            if dz:
                both()
            else:
                pl.when(t > 0)(both)
        for dx in range(1, rows):
            ready(qbuf.at[u, x], s2.at[u, dx])
            ready(pbuf.at[u, add(x, dx, rows)], s3.at[u, dx])
        return carry

    lax.fori_loop(0, units, drain, 0)


def exchange(outgoing, kv_cache, slot_of_unit, live, groups, members):
    units, cands, width = outgoing.shape
    lines = LINE
    rows = members // lines
    cap = units // groups
    count = kv_cache.shape[1]
    smem = pl.BlockSpec(memory_space=pltpu.SMEM)
    vmem = pl.BlockSpec(memory_space=pltpu.VMEM)
    sixteen = jnp.bfloat16
    sem = pltpu.SemaphoreType.DMA
    return pl.pallas_call(
        functools.partial(kernel, (groups, lines, rows, cap)),
        out_shape=jax.ShapeDtypeStruct(outgoing.shape, jnp.float32),
        in_specs=[smem, smem, smem, vmem, pl.BlockSpec(memory_space=pl.ANY)],
        out_specs=vmem,
        scratch_shapes=[
            pltpu.VMEM(kv_cache.shape, sixteen),
            pltpu.VMEM((units, rows, lines, cands, width), sixteen),
            pltpu.VMEM((units, rows, lines, cands, width), sixteen),
            pltpu.VMEM((units, rows, lines, cands, width), sixteen),
            pltpu.VMEM((units, lines, cands, width), sixteen),
            pltpu.VMEM((units, lines, cands, width), sixteen),
            sem,
            sem((units, lines)),
            sem((units, lines)),
            sem((units, rows)),
            sem((units, rows)),
            sem((units, rows)),
            sem((units, rows)),
            sem((units, lines)),
            sem((units, lines)),
        ],
        compiler_params=pltpu.CompilerParams(
            collective_id=0, has_side_effects=True, vmem_limit_bytes=56 * 1024 * 1024
        ),
        cost_estimate=pl.CostEstimate(
            flops=4 * units * cands * members * count * width,
            bytes_accessed=2 * kv_cache.size,
            transcendentals=units * cands * members * count * HEADS,
        ),
    )(slot_of_unit, live, 1.0 / live.astype(jnp.float32), outgoing, kv_cache)


def on_device(candidates, kv_cache, cache_request, rank_request, hist_blocks, w_uq, w_out):
    groups = lax.axis_size("group")
    per_group, count, _ = kv_cache.shape
    cand_rows = candidates.shape[0]
    width = candidates.shape[2]
    head_dim = width // HEADS
    cap = per_group // groups
    group_now = lax.axis_index("group")
    members = lax.axis_size("member")
    target, arrival, slot_of_pos = routing(cache_request, rank_request, per_group)
    first = group_now * per_group
    local = first + jnp.arange(per_group, dtype=jnp.int32)
    source = slot_of_pos[local]
    hops = lax.rem(source // per_group - group_now + groups, groups)
    unit_of_pos = hops * cap + arrival[source]
    pos_of_unit = inverse(unit_of_pos)
    unit_of_slot = lax.rem(group_now - target[local] + groups, groups) * cap + arrival[local]
    slot_of_unit = inverse(unit_of_slot)
    live = hist_blocks[cache_request[local]][slot_of_unit] * BLK

    inputs = candidates.astype(jnp.float32)
    normed = layer_norm(inputs).astype(jnp.bfloat16).reshape(cand_rows * per_group, width)
    projected = jax.nn.silu(jnp.dot(normed, w_uq, preferred_element_type=jnp.float32))
    gates = projected[:, :width].reshape(cand_rows, per_group, width)
    queries = projected[:, width:].astype(jnp.bfloat16).reshape(cand_rows, per_group, width)
    outgoing = jnp.transpose(queries, (1, 0, 2))[pos_of_unit]
    sums = exchange(outgoing, kv_cache, slot_of_unit, live, groups, members)
    attn = jnp.transpose(sums[unit_of_pos], (1, 0, 2))
    gated = (layer_norm(attn) * gates).astype(jnp.bfloat16).reshape(cand_rows * per_group, width)
    result = jnp.dot(gated, w_out, preferred_element_type=jnp.float32) + inputs.reshape(
        cand_rows * per_group, width
    )
    return result.astype(jnp.bfloat16).reshape(cand_rows, per_group, width)


def solution(mesh):
    return jax.shard_map(
        on_device,
        mesh=mesh,
        in_specs=(P("member", "group", None), P("group", "member", None), P(), P(), P(), P(), P()),
        out_specs=P("member", "group", None),
        check_vma=False,
    )
```

time: 395 us -> 254 us (0.64); the launches traced: 390 us -> 254 us
  waiting for transfers between devices: 273 us -> 0 us
  Pallas kernels: 0 us -> 222 us
  local copies, waits for them, and re-layouts: 58.9 us -> 15.4 us
  matrix products: 27 us -> 7.46 us
  between operations: 13.6 us -> 0.22 us
  starting transfers between devices: 8.82 us -> 0 us
    pallas_call x0 -> x1, Pallas kernels: none -> 222 us  [exchange(): pl.pallas_call(functools.partial(kernel, (groups, lines, rows, cap)), out...]
    reduce_scatter x1 -> x0, waiting for transfers between devices: 147 us -> none  [on_device(): lax.psum_scatter(partial, 'member', scatter_dimension=1, tiled=True)]
    all_gather x1 -> x0, waiting for transfers between devices: 103 us -> none  [on_device(): every = lax.all_gather(incoming, 'member', axis=1, tiled=True)]
    all_to_all x2 -> x0, waiting for transfers between devices: 22.8 us -> none  [the longest x1 12.3 us: on_device(): lax.all_to_all(outgoing, 'group', split_axis=0, concat_axis=0, tiled=True)]
    dot_general x1 -> x0, matrix products: 19.2 us -> none  [on_device(): jnp.einsum('rhce,rehd->rchd', weights, values, preferred_element_type=jnp...]
    slice x2 -> x0, local copies, waits for them, and re-layouts: 12.4 us -> none  [the longest x1 6.49 us: on_device(): values = kv_cache[:, :, width:].reshape(per_group, count, HEADS, head_dim)]
    reshape x1 -> x0, local copies, waits for them, and re-layouts: 11.4 us -> none  [on_device(): partial.astype(jnp.bfloat16).reshape(per_group, every.shape[1], width)]
    all_gather x1 -> x0, local copies, waits for them, and re-layouts: 11.4 us -> none  [on_device(): every = lax.all_gather(incoming, 'member', axis=1, tiled=True)]
  transfers between devices with their start and end apart: 4 -> 0, of which waited for: 4 -> 0; matrix products, arithmetic and copies ran while one was open for 6% -> 0% of each run, Pallas kernels for 0% -> 0%
where the time goes in v2:
time: 254 us
  Pallas kernels  222 us (87%)
  local copies, waits for them, and re-layouts  15.4 us (6%)
  other arithmetic  8.65 us (3%)
  matrix products  7.46 us (3%)
    pallas_call x1, Pallas kernels, exchange(): pl.pallas_call(functools.partial(kernel, (groups, lines, rows, cap)), out...  222 us

profile of v2, /device:TPU:25, one launch (start us, length us, event | category | flops | bytes accessed | tf_op | source)
XLA Modules:
  0.0 254.1 jit_solution(1389535646276020737)
XLA Ops:
  0.0 1.6 convert_reduce_fusion
  1.6 0.1 copy.32
  1.7 0.1 copy.33
  1.8 1.6 fusion.2
  3.5 0.1 copy.35
  3.6 5.0 %divide_multiply_fusion = f32[512,2048]{1,0:T(8,128)S(1)} fusion(bf16[1024,2048]{1,0:T(8,128)(2,1)} %param.12, bf16[64,8,1024]{2,1,0:T(8,128)(2,1)S(1)} %copy-done.5, f32[64,8]{1,0:T(8,128)S(1)} %copy.35, f32[64,8]{1,0:T(8,128)S(1)} %copy.33), kind=kOutput, calls=%fused_computation.9 | convolution fusion | flops 2153775104 | bytes 9441280 | tf_op jit(solution)/shard_map/dot_general | solution.py:298
  8.7 1.6 slice_bitcast_fusion
  10.2 0.9 copy-done.7
  11.2 0.2 fusion.19
  11.4 0.2 convert_reduce_fusion.1
  11.6 0.6 gather_fusion.1
  12.2 0.6 gather_fusion
  12.9 0.1 select_reduce_fusion.1.slot_ref
  13.0 0.6 gather_fusion.2
  13.7 0.6 gather_fusion.3
  14.4 0.6 gather_fusion.4
  15.0 0.5 broadcast_multiply_fusion.2.live_ref
  15.6 0.6 convert_divide_fusion.share_ref
  16.1 1.7 fusion.8
  17.9 0.6 copy.47
  18.5 0.6 gather_fusion.5
  19.1 0.6 gather_fusion.6
  19.8 0.1 select_reduce_fusion
  19.9 1.6 gather_fusion.7
  21.5 222.4 %shard_map.73 = f32[8,64,1024]{2,1,0:T(8,128)} custom-call(s32[8]{0:T(128)} %copy-done.9, s32[8]{0:T(128)} %broadcast_multiply_fusion.2.live_ref, f32[8]{0:T(128)} %convert_divide_fusion.share_ref, bf16[8,64,1024]{2,1,0:T(8,128)(2,1)} %gather_fusion.7, bf16[8,256,2048]{2,1,0:T(8,128)(2,1)} %kv_hbm.1), custom_call_target="tpu_custom_call" | custom-call | flops 4294967296 | bytes 8388608 | tf_op jit(solution)/shard_map/pallas_call | solution.py:243
  244.0 3.6 %gather_fusion.8 = f32[8,64,1024]{2,1,0:T(8,128)} fusion(f32[8,64,1024]{2,1,0:T(8,128)} %shard_map.73, s32[1024]{0:T(1024)S(1)} %pad_clamp_fusion), kind=kCustom, calls=%fused_computation.8 | custom fusion | bytes 4194336 | tf_op jit(solution)/shard_map/gather | solution.py:303
  247.6 1.9 bitcast_reduce_fusion
  249.5 0.3 copy-done.3
  249.8 0.3 multiply_reduce_fusion
  250.1 0.3 copy-done.4
  250.4 1.3 fusion.6
  251.7 2.4 fusion.7
  (37 shorter events, 0.3 us)
Async XLA Ops:
  0.0 251.7 %copy-start = (bf16[1024,1024]{1,0:T(8,128)(2,1)S(1)}, bf16[1024,1024]{1,0:T(8,128)(2,1)}, u32[]{:S(2)}) copy-start(bf16[1024,1024]{1,0:T(8,128)(2,1)} %param.13) | copy-start | bytes 6291460
  0.0 3.6 %copy-start.5 = (bf16[64,8,1024]{2,1,0:T(8,128)(2,1)S(1)}, bf16[64,8,1024]{2,1,0:T(8,128)(2,1)}, u32[]{:S(2)}) copy-start(bf16[64,8,1024]{2,1,0:T(8,128)(2,1)} %param.7) | copy-start | bytes 3145732
  8.6 2.6 %copy-start.7 = (f32[512,2048]{1,0:T(8,128)}, f32[512,2048]{1,0:T(8,128)S(1)}, u32[]{:S(2)}) copy-start(f32[512,2048]{1,0:T(8,128)S(1)} %divide_multiply_fusion) | copy-start | bytes 12582916
  8.6 2.6 %copy-start.1 = (s32[32]{0:T(128)S(1)}, s32[32]{0:T(128)}, u32[]{:S(2)}) copy-start(s32[32]{0:T(128)} %param.9) | copy-start | bytes 388
  8.6 2.5 %copy-start.8 = (s32[32]{0:T(128)S(1)}, s32[32]{0:T(128)}, u32[]{:S(2)}) copy-start(s32[32]{0:T(128)} %param.10) | copy-start | bytes 388
  8.6 5.0 %copy-start.2 = (s32[32]{0:T(128)S(1)}, s32[32]{0:T(128)}, u32[]{:S(2)}) copy-start(s32[32]{0:T(128)} %param.11) | copy-start | bytes 388
  13.0 5.5 %copy-start.9 = (s32[8]{0:T(128)}, s32[8]{0:T(128)S(1)}, u32[]{:S(2)}) copy-start(s32[8]{0:T(128)S(1)} %select_reduce_fusion.1.slot_ref) | copy-start | bytes 100
  247.6 2.2 copy-start.3
  247.6 2.9 %copy-start.4 = (f32[64,8,1024]{2,1,0:T(8,128)S(1)}, f32[64,8,1024]{2,1,0:T(8,128)}, u32[]{:S(2)}) copy-start(f32[64,8,1024]{2,1,0:T(8,128)} %slice_bitcast_fusion) | copy-start | bytes 6291460
  250.4 1.3 copy-start.6

commit v3 on v2

--- a/solution.py
+++ b/solution.py
@@ -18,7 +18,9 @@
     return center * lax.rsqrt(spread + 1e-05)
 
 
-def routing(cache_request, rank_request, per_group):
+def routing(cache_request, rank_request, hist_blocks, per_group, groups, group_now):
+    cap = per_group // groups
+    first = group_now * per_group
     slot_ids = jnp.arange(cache_request.shape[0], dtype=jnp.int32)
     match = cache_request[:, None] == rank_request[None, :]
     rank_pos = jnp.sum(jnp.where(match, slot_ids[None, :], 0), axis=1)
@@ -30,8 +32,25 @@
         & (slot_ids[None, :] < slot_ids[:, None])
     )
     arrival = jnp.sum(earlier.astype(jnp.int32), axis=1)
-    slot_of_pos = jnp.sum(jnp.where(match, slot_ids[:, None], 0), axis=0)
-    return (target, arrival, slot_of_pos)
+    leaving = lax.rem(owner_grp - group_now + groups, groups) * cap + arrival
+    arriving = lax.rem(group_now - target + groups, groups) * cap + arrival
+    ids = jnp.arange(per_group, dtype=jnp.int32)
+    ranked_here = lax.dynamic_slice_in_dim(rank_request, first, per_group)
+    unit_of_pos = jnp.sum(
+        jnp.where(cache_request[:, None] == ranked_here[None, :], leaving[:, None], 0), axis=0
+    )
+    mine = owner_grp == group_now
+    slot_of_unit = jnp.sum(
+        jnp.where(
+            mine[:, None] & (arriving[:, None] == ids[None, :]), (slot_ids - first)[:, None], 0
+        ),
+        axis=0,
+    )
+    cached_here = lax.dynamic_slice_in_dim(cache_request, first, per_group)
+    blocks = jnp.sum(
+        jnp.where(slot_ids[:, None] == cached_here[None, :], hist_blocks[:, None], 0), axis=0
+    )
+    return unit_of_pos, inverse(unit_of_pos), slot_of_unit, blocks * BLK
 
 
 def inverse(order):
@@ -41,12 +60,15 @@
 
 def kernel(
     dims,
+    pos_ref,
+    unit_ref,
     slot_ref,
     live_ref,
     share_ref,
     q_ref,
     kv_hbm,
     out_ref,
+    qown,
     kv,
     qbuf,
     pbuf,
@@ -108,10 +130,11 @@
 
     def scatter_queries(u, carry):
         t = u // cap
+        qown[u] = q_ref[pos_ref[u]]
         for dz in range(lines):
             there = (add(g, t, groups), add(z, dz, lines), x)
             send = lambda: remote(
-                q_ref.at[u], qbuf.at[u, x, z], s1.at[u, dz], r1.at[u, dz], at(*there)
+                qown.at[u], qbuf.at[u, x, z], s1.at[u, dz], r1.at[u, dz], at(*there)
             ).start()
             if dz:
                 send()
@@ -119,32 +142,34 @@
                 pl.when(t > 0)(send)
                 pl.when(t == 0)(
                     lambda: pltpu.make_async_copy(
-                        q_ref.at[u], qbuf.at[u, x, z], r1.at[u, 0]
+                        qown.at[u], qbuf.at[u, x, z], r1.at[u, 0]
                     ).start()
                 )
         return carry
 
     lax.fori_loop(0, units, scatter_queries, 0)
-    panel.wait()
 
     def forward(u):
         for dz in range(lines):
-            ready(qbuf.at[u, x, add(z, lines - dz, lines)], r1.at[u, dz])
-        for dx in range(1, rows):
-            remote(
-                qbuf.at[u, x],
-                qbuf.at[u, x],
-                s2.at[u, dx],
-                r2.at[u, dx],
-                at(g, z, add(x, dx, rows)),
-            ).start()
+            line = add(z, lines - dz, lines)
+            ready(qbuf.at[u, x, line], r1.at[u, dz])
+            for dx in range(1, rows):
+                remote(
+                    qbuf.at[u, x, line],
+                    qbuf.at[u, x, line],
+                    s2.at[u, dx, dz],
+                    r2.at[u, dx, dz],
+                    at(g, z, add(x, dx, rows)),
+                ).start()
 
     def attend(u):
         for dx in range(1, rows):
-            ready(qbuf.at[u, add(x, rows - dx, rows)], r2.at[u, dx])
+            for dz in range(lines):
+                line = add(z, lines - dz, lines)
+                ready(qbuf.at[u, add(x, rows - dx, rows), line], r2.at[u, dx, dz])
         slot = slot_ref[u]
-        limit = live_ref[u] - member * count
-        share = share_ref[u]
+        limit = live_ref[slot] - member * count
+        share = share_ref[slot]
         keep = lax.broadcasted_iota(jnp.int32, (count, head_dim), 0) < limit
         keep = keep.astype(jnp.float32)
         for h in range(HEADS):
@@ -194,19 +219,26 @@
 
     def stage(i, carry):
         pl.when(i < units)(lambda: forward(i))
+        pl.when(i == 1)(panel.wait)
         pl.when((i >= 1) & (i < units + 1))(lambda: attend(i - 1))
         pl.when(i >= 2)(lambda: give_back(i - 2))
         return carry
 
     lax.fori_loop(0, units + 2, stage, 0)
 
-    def collect(u, carry):
+    def arrived(u, carry):
         for dz in range(lines):
             ready(fin.at[u, dz], r4.at[u, dz])
+        return carry
+
+    lax.fori_loop(0, units, arrived, 0)
+
+    def collect(p, carry):
+        u = unit_ref[p]
         total = fin[u, 0].astype(jnp.float32)
         for dz in range(1, lines):
             total = total + fin[u, dz].astype(jnp.float32)
-        out_ref[u] = total
+        out_ref[p] = total
         return carry
 
     lax.fori_loop(0, units, collect, 0)
@@ -215,7 +247,7 @@
         t = u // cap
         for dz in range(lines):
             def both():
-                ready(q_ref.at[u], s1.at[u, dz])
+                ready(qown.at[u], s1.at[u, dz])
                 ready(ssum.at[u, add(z, dz, lines)], s4.at[u, dz])
 
             if dz:
@@ -223,15 +255,16 @@
             else:
                 pl.when(t > 0)(both)
         for dx in range(1, rows):
-            ready(qbuf.at[u, x], s2.at[u, dx])
+            for dz in range(lines):
+                ready(qbuf.at[u, x, add(z, lines - dz, lines)], s2.at[u, dx, dz])
             ready(pbuf.at[u, add(x, dx, rows)], s3.at[u, dx])
         return carry
 
     lax.fori_loop(0, units, drain, 0)
 
 
-def exchange(outgoing, kv_cache, slot_of_unit, live, groups, members):
-    units, cands, width = outgoing.shape
+def exchange(routes, queries, kv_cache, groups, members):
+    units, cands, width = queries.shape
     lines = LINE
     rows = members // lines
     cap = units // groups
@@ -242,10 +275,11 @@
     sem = pltpu.SemaphoreType.DMA
     return pl.pallas_call(
         functools.partial(kernel, (groups, lines, rows, cap)),
-        out_shape=jax.ShapeDtypeStruct(outgoing.shape, jnp.float32),
-        in_specs=[smem, smem, smem, vmem, pl.BlockSpec(memory_space=pl.ANY)],
+        out_shape=jax.ShapeDtypeStruct(queries.shape, jnp.float32),
+        in_specs=[smem] * 5 + [vmem, pl.BlockSpec(memory_space=pl.ANY)],
         out_specs=vmem,
         scratch_shapes=[
+            pltpu.VMEM(queries.shape, sixteen),
             pltpu.VMEM(kv_cache.shape, sixteen),
             pltpu.VMEM((units, rows, lines, cands, width), sixteen),
             pltpu.VMEM((units, rows, lines, cands, width), sixteen),
@@ -255,8 +289,8 @@
             sem,
             sem((units, lines)),
             sem((units, lines)),
-            sem((units, rows)),
-            sem((units, rows)),
+            sem((units, rows, lines)),
+            sem((units, rows, lines)),
             sem((units, rows)),
             sem((units, rows)),
             sem((units, lines)),
@@ -270,42 +304,32 @@
             bytes_accessed=2 * kv_cache.size,
             transcendentals=units * cands * members * count * HEADS,
         ),
-    )(slot_of_unit, live, 1.0 / live.astype(jnp.float32), outgoing, kv_cache)
+    )(*routes, queries, kv_cache)
 
 
 def on_device(candidates, kv_cache, cache_request, rank_request, hist_blocks, w_uq, w_out):
     groups = lax.axis_size("group")
-    per_group, count, _ = kv_cache.shape
+    per_group = kv_cache.shape[0]
     cand_rows = candidates.shape[0]
     width = candidates.shape[2]
-    head_dim = width // HEADS
-    cap = per_group // groups
     group_now = lax.axis_index("group")
     members = lax.axis_size("member")
-    target, arrival, slot_of_pos = routing(cache_request, rank_request, per_group)
-    first = group_now * per_group
-    local = first + jnp.arange(per_group, dtype=jnp.int32)
-    source = slot_of_pos[local]
-    hops = lax.rem(source // per_group - group_now + groups, groups)
-    unit_of_pos = hops * cap + arrival[source]
-    pos_of_unit = inverse(unit_of_pos)
-    unit_of_slot = lax.rem(group_now - target[local] + groups, groups) * cap + arrival[local]
-    slot_of_unit = inverse(unit_of_slot)
-    live = hist_blocks[cache_request[local]][slot_of_unit] * BLK
-
-    inputs = candidates.astype(jnp.float32)
-    normed = layer_norm(inputs).astype(jnp.bfloat16).reshape(cand_rows * per_group, width)
+    unit_of_pos, pos_of_unit, slot_of_unit, live = routing(
+        cache_request, rank_request, hist_blocks, per_group, groups, group_now
+    )
+    inputs = jnp.transpose(candidates, (1, 0, 2)).astype(jnp.float32)
+    normed = layer_norm(inputs).astype(jnp.bfloat16).reshape(per_group * cand_rows, width)
     projected = jax.nn.silu(jnp.dot(normed, w_uq, preferred_element_type=jnp.float32))
-    gates = projected[:, :width].reshape(cand_rows, per_group, width)
-    queries = projected[:, width:].astype(jnp.bfloat16).reshape(cand_rows, per_group, width)
-    outgoing = jnp.transpose(queries, (1, 0, 2))[pos_of_unit]
-    sums = exchange(outgoing, kv_cache, slot_of_unit, live, groups, members)
-    attn = jnp.transpose(sums[unit_of_pos], (1, 0, 2))
+    gates = projected[:, :width].reshape(per_group, cand_rows, width)
+    queries = projected[:, width:].astype(jnp.bfloat16).reshape(per_group, cand_rows, width)
+    routes = (pos_of_unit, unit_of_pos, slot_of_unit, live, 1.0 / live.astype(jnp.float32))
+    attn = exchange(routes, queries, kv_cache, groups, members)
     gated = (layer_norm(attn) * gates).astype(jnp.bfloat16).reshape(cand_rows * per_group, width)
     result = jnp.dot(gated, w_out, preferred_element_type=jnp.float32) + inputs.reshape(
         cand_rows * per_group, width
     )
-    return result.astype(jnp.bfloat16).reshape(cand_rows, per_group, width)
+    result = result.astype(jnp.bfloat16).reshape(per_group, cand_rows, width)
+    return jnp.transpose(result, (1, 0, 2))
 
 
 def solution(mesh):

time: 254 us -> 246 us (0.969)
  local copies, waits for them, and re-layouts: 15.4 us -> 7.34 us
  other arithmetic: 8.65 us -> 16.3 us
  Pallas kernels: 222 us -> 218 us
  matrix products: 7.46 us -> 4.08 us
    gather x9 -> x0, local copies, waits for them, and re-layouts: 9.66 us -> none  [the longest x1 3.57 us: on_device(): attn = jnp.transpose(sums[unit_of_pos], (1, 0, 2))]
    pallas_call x1, Pallas kernels: 222 us -> 218 us  [exchange(): pl.pallas_call(functools.partial(kernel, (groups, lines, rows, cap)), out...]
    reduce_sum x1 -> x4, other arithmetic: 0.18 us -> 3.39 us  [the longest x1 1.01 us: routing(): rank_pos = jnp.sum(jnp.where(match, slot_ids[None, :], 0), axis=1)]
    slice x0 -> x2, local copies, waits for them, and re-layouts: none -> 2.62 us  [the longest x1 1.49 us: on_device(): gates = projected[:, :width].reshape(per_group, cand_rows, width)]
where the time goes in v3:
time: 246 us
  Pallas kernels  218 us (89%)
  other arithmetic  16.3 us (7%)
  local copies, waits for them, and re-layouts  7.34 us (3%)
  matrix products  4.08 us (2%)
    pallas_call x1, Pallas kernels, exchange(): pl.pallas_call(functools.partial(kernel, (groups, lines, rows, cap)), out...  218 us

profile of v3, /device:TPU:25, one launch (start us, length us, event | category | flops | bytes accessed | tf_op | source)
XLA Modules:
  0.0 246.0 jit_solution(14565629967358652428)
XLA Ops:
  0.0 0.0 copy-start
  0.0 0.0 copy-start.2
  0.0 1.0 select_reduce_fusion
  1.0 0.7 dynamic_slice.6
  1.8 0.7 dynamic_slice.7
  2.5 0.8 select_reduce_fusion.1
  3.3 0.6 convert_divide_fusion.share_ref
  3.9 0.5 broadcast_multiply_fusion.2.live_ref
  4.4 0.2 convert_reduce_fusion
  4.6 0.7 select_reduce_fusion.2.slot_ref
  5.3 0.8 select_reduce_fusion.4.unit_ref
  6.1 0.7 select_reduce_fusion.3.pos_ref
  6.8 2.1 bitcast_reduce_fusion
  8.9 2.3 fusion.3
  11.3 0.0 copy-done.2
  11.3 0.6 fusion.4
  11.9 0.0 copy-done.4
  11.9 1.5 copy.14
  13.5 0.0 copy-done.5
  13.5 2.8 %divide_multiply_fusion = f32[512,2048]{1,0:T(8,128)S(1)} fusion(bf16[512,1024]{1,0:T(8,128)(2,1)S(1)} %bitcast.31, bf16[1024,2048]{1,0:T(8,128)(2,1)S(1)} %copy-done.5), kind=kOutput, calls=%fused_computation | convolution fusion | flops 2151677952 | bytes 9437184 | tf_op jit(solution)/shard_map/dot_general | solution.py:322
  16.3 1.1 slice.12
  17.5 1.5 slice.10
  18.9 218.2 %shard_map.73 = f32[8,64,1024]{2,1,0:T(8,128)} custom-call(s32[8]{0:T(128)} %select_reduce_fusion.3.pos_ref, s32[8]{0:T(128)} %copy-done.4, s32[8]{0:T(128)} %select_reduce_fusion.2.slot_ref, s32[8]{0:T(128)} %broadcast_multiply_fusion.2.live_ref, f32[8]{0:T(128)} %convert_divide_fusion.share_ref, bf16[8,64,1024]{2,1,0:T(8,128)(2,1)} %bitcast.30, ...), custom_call_target="tpu_custom_call" | custom-call | flops 4294967296 | bytes 8388608 | tf_op jit(solution)/shard_map/pallas_call | solution.py:276
  237.2 1.8 reduce_sum.98
  238.9 0.0 copy-start.1
  239.0 2.1 multiply_reduce_fusion
  241.0 0.1 copy-done.1
  241.2 2.0 multiply_convert_fusion
  243.2 0.0 copy-done
  243.2 0.0 copy-done.3
  243.2 1.3 fusion
  244.5 1.5 copy.20
  (11 shorter events, 0.1 us)
Async XLA Ops:
  0.0 243.2 %copy-start = (bf16[1024,1024]{1,0:T(8,128)(2,1)S(1)}, bf16[1024,1024]{1,0:T(8,128)(2,1)}, u32[]{:S(2)}) copy-start(bf16[1024,1024]{1,0:T(8,128)(2,1)} %param.13) | copy-start | bytes 6291460
  0.0 11.3 %copy-start.2 = (bf16[64,8,1024]{2,1,0:T(8,128)(2,1)S(1)}, bf16[64,8,1024]{2,1,0:T(8,128)(2,1)}, u32[]{:S(2)}) copy-start(bf16[64,8,1024]{2,1,0:T(8,128)(2,1)} %param.7) | copy-start | bytes 3145732
  6.1 5.8 %copy-start.4 = (s32[8]{0:T(128)}, s32[8]{0:T(128)S(1)}, u32[]{:S(2)}) copy-start(s32[8]{0:T(128)S(1)} %select_reduce_fusion.4.unit_ref) | copy-start | bytes 100
  11.3 2.2 copy-start.5
  238.9 2.2 copy-start.1
  241.2 2.1 copy-start.3

commit v4 on v3

--- a/solution.py
+++ b/solution.py
@@ -10,6 +10,7 @@
 HEADS = 8
 BLK = 128
 LINE = 4
+AHEAD = 2
 
 
 def layer_norm(values):
@@ -18,7 +19,7 @@
     return center * lax.rsqrt(spread + 1e-05)
 
 
-def routing(cache_request, rank_request, hist_blocks, per_group, groups, group_now):
+def routing(cache_request, rank_request, per_group, groups, group_now):
     cap = per_group // groups
     first = group_now * per_group
     slot_ids = jnp.arange(cache_request.shape[0], dtype=jnp.int32)
@@ -35,27 +36,12 @@
     leaving = lax.rem(owner_grp - group_now + groups, groups) * cap + arrival
     arriving = lax.rem(group_now - target + groups, groups) * cap + arrival
     ids = jnp.arange(per_group, dtype=jnp.int32)
-    ranked_here = lax.dynamic_slice_in_dim(rank_request, first, per_group)
-    unit_of_pos = jnp.sum(
-        jnp.where(cache_request[:, None] == ranked_here[None, :], leaving[:, None], 0), axis=0
-    )
-    mine = owner_grp == group_now
-    slot_of_unit = jnp.sum(
-        jnp.where(
-            mine[:, None] & (arriving[:, None] == ids[None, :]), (slot_ids - first)[:, None], 0
-        ),
-        axis=0,
-    )
-    cached_here = lax.dynamic_slice_in_dim(cache_request, first, per_group)
-    blocks = jnp.sum(
-        jnp.where(slot_ids[:, None] == cached_here[None, :], hist_blocks[:, None], 0), axis=0
-    )
-    return unit_of_pos, inverse(unit_of_pos), slot_of_unit, blocks * BLK
-
-
-def inverse(order):
-    ids = jnp.arange(order.shape[0], dtype=jnp.int32)
-    return jnp.sum(jnp.where(order[None, :] == ids[:, None], ids[None, :], 0), axis=1)
+    unit_of_pos = jnp.sum(jnp.where(match, leaving[:, None], 0), axis=0)
+    ranks = (target == group_now)[:, None] & (leaving[:, None] == ids[None, :])
+    pos_of_unit = jnp.sum(jnp.where(ranks, (rank_pos - first)[:, None], 0), axis=0)
+    holds = (owner_grp == group_now)[:, None] & (arriving[:, None] == ids[None, :])
+    slot_of_unit = jnp.sum(jnp.where(holds, (slot_ids - first)[:, None], 0), axis=0)
+    return pos_of_unit, unit_of_pos, slot_of_unit
 
 
 def kernel(
@@ -63,8 +49,8 @@
     pos_ref,
     unit_ref,
     slot_ref,
-    live_ref,
-    share_ref,
+    cache_ref,
+    blocks_ref,
     q_ref,
     kv_hbm,
     out_ref,
@@ -128,7 +114,7 @@
             device_id_type=pl.DeviceIdType.MESH,
         )
 
-    def scatter_queries(u, carry):
+    def scatter_queries(u, carry=0):
         t = u // cap
         qown[u] = q_ref[pos_ref[u]]
         for dz in range(lines):
@@ -147,7 +133,7 @@
                 )
         return carry
 
-    lax.fori_loop(0, units, scatter_queries, 0)
+    lax.fori_loop(0, min(AHEAD, units), scatter_queries, 0)
 
     def forward(u):
         for dz in range(lines):
@@ -168,8 +154,10 @@
                 line = add(z, lines - dz, lines)
                 ready(qbuf.at[u, add(x, rows - dx, rows), line], r2.at[u, dx, dz])
         slot = slot_ref[u]
-        limit = live_ref[slot] - member * count
-        share = share_ref[slot]
+        live = blocks_ref[cache_ref[g * units + slot]] * BLK
+        limit = live - member * count
+        share = 1.0 / jnp.full((8, head_dim), live, jnp.int32).astype(jnp.float32)
+        share = share[0:1, :]
         keep = lax.broadcasted_iota(jnp.int32, (count, head_dim), 0) < limit
         keep = keep.astype(jnp.float32)
         for h in range(HEADS):
@@ -217,8 +205,12 @@
                     ).start()
                 )
 
+    def later(u):
+        scatter_queries(u)
+
     def stage(i, carry):
         pl.when(i < units)(lambda: forward(i))
+        pl.when(i + AHEAD < units)(lambda: later(i + AHEAD))
         pl.when(i == 1)(panel.wait)
         pl.when((i >= 1) & (i < units + 1))(lambda: attend(i - 1))
         pl.when(i >= 2)(lambda: give_back(i - 2))
@@ -234,11 +226,11 @@
     lax.fori_loop(0, units, arrived, 0)
 
     def collect(p, carry):
-        u = unit_ref[p]
+        u = unit_ref[g * units + p]
         total = fin[u, 0].astype(jnp.float32)
         for dz in range(1, lines):
             total = total + fin[u, dz].astype(jnp.float32)
-        out_ref[p] = total
+        out_ref[p] = layer_norm(total)
         return carry
 
     lax.fori_loop(0, units, collect, 0)
@@ -314,17 +306,15 @@
     width = candidates.shape[2]
     group_now = lax.axis_index("group")
     members = lax.axis_size("member")
-    unit_of_pos, pos_of_unit, slot_of_unit, live = routing(
-        cache_request, rank_request, hist_blocks, per_group, groups, group_now
-    )
+    routes = routing(cache_request, rank_request, per_group, groups, group_now)
+    routes += (cache_request, hist_blocks)
     inputs = jnp.transpose(candidates, (1, 0, 2)).astype(jnp.float32)
     normed = layer_norm(inputs).astype(jnp.bfloat16).reshape(per_group * cand_rows, width)
     projected = jax.nn.silu(jnp.dot(normed, w_uq, preferred_element_type=jnp.float32))
     gates = projected[:, :width].reshape(per_group, cand_rows, width)
     queries = projected[:, width:].astype(jnp.bfloat16).reshape(per_group, cand_rows, width)
-    routes = (pos_of_unit, unit_of_pos, slot_of_unit, live, 1.0 / live.astype(jnp.float32))
     attn = exchange(routes, queries, kv_cache, groups, members)
-    gated = (layer_norm(attn) * gates).astype(jnp.bfloat16).reshape(cand_rows * per_group, width)
+    gated = (attn * gates).astype(jnp.bfloat16).reshape(cand_rows * per_group, width)
     result = jnp.dot(gated, w_out, preferred_element_type=jnp.float32) + inputs.reshape(
         cand_rows * per_group, width
     )

time: 246 us -> 237 us (0.963)
  other arithmetic: 16.3 us -> 9.41 us
  local copies, waits for them, and re-layouts: 7.34 us -> 4.85 us
where the time goes in v4:
time: 237 us
  Pallas kernels  216 us (91%)
  other arithmetic  9.41 us (4%)
  matrix products  6.23 us (3%)
  local copies, waits for them, and re-layouts  4.85 us (2%)
    pallas_call x1, Pallas kernels, exchange(): pl.pallas_call(functools.partial(kernel, (groups, lines, rows, cap)), out...  216 us
    dot_general x1, matrix products, on_device(): jnp.dot(normed, w_uq, preferred_element_type=jnp.float32)  4.97 us

profile of v4, /device:TPU:25, one launch (start us, length us, event | category | flops | bytes accessed | tf_op | source)
XLA Modules:
  0.0 236.7 jit_solution(15070790607323179541)
XLA Ops:
  0.0 0.0 copy-start
  0.0 0.0 copy-start.1
  0.0 1.0 fusion.5
  1.0 0.2 convert_reduce_fusion
  1.3 0.6 select_reduce_fusion.1.pos_ref
  1.9 0.6 select_reduce_fusion.slot_ref
  2.5 1.3 fusion.6.unit_ref
  3.8 2.1 bitcast_reduce_fusion
  6.0 2.3 fusion.3
  8.3 0.0 copy-done.1
  8.3 0.6 fusion.4
  8.9 5.0 %divide_multiply_fusion = f32[512,2048]{1,0:T(8,128)S(1)} fusion(bf16[512,1024]{1,0:T(8,128)(2,1)S(1)} %bitcast.31, bf16[1024,2048]{1,0:T(8,128)(2,1)} %param.12), kind=kOutput, calls=%fused_computation | convolution fusion | flops 2151677952 | bytes 9437184 | tf_op jit(solution)/shard_map/dot_general | solution.py:313
  13.9 1.1 slice.12
  15.1 216.1 %shard_map.73 = f32[8,64,1024]{2,1,0:T(8,128)} custom-call(s32[8]{0:T(128)} %select_reduce_fusion.1.pos_ref, s32[32]{0:T(128)} %fusion.6.unit_ref, s32[8]{0:T(128)} %select_reduce_fusion.slot_ref, s32[32]{0:T(128)} %cache_ref.1, s32[32]{0:T(128)} %blocks_ref.1, bf16[8,64,1024]{2,1,0:T(8,128)(2,1)} %bitcast.30, bf16[8,256,2048]{2,1,0:T(8,128)(2,1)} %kv_hbm.1), custom_call_target="tpu_custom_call" | custom-call | flops 4294967296 | bytes 8388608 | tf_op jit(solution)/shard_map/pallas_call | solution.py:268
  231.2 0.0 copy-start.2
  231.2 0.1 slice.10
  231.4 1.4 copy-done.2
  232.8 0.5 multiply_convert_fusion
  233.3 0.6 copy.12
  233.9 0.0 copy-done
  233.9 1.3 fusion
  235.2 1.5 copy.18
  (6 shorter events, 0.1 us)
Async XLA Ops:
  0.0 233.9 %copy-start = (bf16[1024,1024]{1,0:T(8,128)(2,1)S(1)}, bf16[1024,1024]{1,0:T(8,128)(2,1)}, u32[]{:S(2)}) copy-start(bf16[1024,1024]{1,0:T(8,128)(2,1)} %param.13) | copy-start | bytes 6291460
  0.0 8.3 %copy-start.1 = (bf16[64,8,1024]{2,1,0:T(8,128)(2,1)S(1)}, bf16[64,8,1024]{2,1,0:T(8,128)(2,1)}, u32[]{:S(2)}) copy-start(bf16[64,8,1024]{2,1,0:T(8,128)(2,1)} %param.7) | copy-start | bytes 3145732
  231.2 1.6 copy-start.2

commit v5 on v4

--- a/solution.py
+++ b/solution.py
@@ -70,6 +70,8 @@
     r3,
     s4,
     r4,
+    s5,
+    r5,
 ):
     groups, lines, rows, cap = dims
     units = groups * cap
@@ -114,6 +116,11 @@
             device_id_type=pl.DeviceIdType.MESH,
         )
 
+    def direct(u):
+        return lax.rem(u, 2) == 1
+
+    mate = z + 1 - 2 * lax.rem(z, 2)
+
     def scatter_queries(u, carry=0):
         t = u // cap
         qown[u] = q_ref[pos_ref[u]]
@@ -122,7 +129,9 @@
             send = lambda: remote(
                 qown.at[u], qbuf.at[u, x, z], s1.at[u, dz], r1.at[u, dz], at(*there)
             ).start()
-            if dz:
+            if dz % 2:
+                pl.when(direct(u))(send)
+            elif dz:
                 send()
             else:
                 pl.when(t > 0)(send)
@@ -137,22 +146,54 @@
 
     def forward(u):
         for dz in range(lines):
+            def pass_on():
+                line = add(z, lines - dz, lines)
+                ready(qbuf.at[u, x, line], r1.at[u, dz])
+                for dx in range(1, rows):
+                    remote(
+                        qbuf.at[u, x, line],
+                        qbuf.at[u, x, line],
+                        s2.at[u, dx, dz],
+                        r2.at[u, dx, dz],
+                        at(g, z, add(x, dx, rows)),
+                    ).start()
+
+            if dz % 2:
+                pl.when(direct(u))(pass_on)
+            else:
+                pass_on()
+
+    def crossed(u, dz):
+        for dx in range(1, rows):
             line = add(z, lines - dz, lines)
-            ready(qbuf.at[u, x, line], r1.at[u, dz])
-            for dx in range(1, rows):
-                remote(
-                    qbuf.at[u, x, line],
-                    qbuf.at[u, x, line],
-                    s2.at[u, dx, dz],
-                    r2.at[u, dx, dz],
-                    at(g, z, add(x, dx, rows)),
-                ).start()
+            ready(qbuf.at[u, add(x, rows - dx, rows), line], r2.at[u, dx, dz])
+
+    def swap(u):
+        for dz in range(0, lines, 2):
+            line = add(z, lines - dz, lines)
+            crossed(u, dz)
+            remote(
+                qbuf.at[u, :, line],
+                qbuf.at[u, :, line],
+                s5.at[u, dz],
+                r5.at[u, dz],
+                at(g, mate, x),
+            ).start()
+
+    def gathered(u):
+        def whole():
+            for dz in range(lines):
+                crossed(u, dz)
+
+        def halves():
+            for dz in range(0, lines, 2):
+                ready(qbuf.at[u, :, add(mate, lines - dz, lines)], r5.at[u, dz])
+
+        pl.when(direct(u))(whole)
+        pl.when(jnp.logical_not(direct(u)))(halves)
 
     def attend(u):
-        for dx in range(1, rows):
-            for dz in range(lines):
-                line = add(z, lines - dz, lines)
-                ready(qbuf.at[u, add(x, rows - dx, rows), line], r2.at[u, dx, dz])
+        gathered(u)
         slot = slot_ref[u]
         live = blocks_ref[cache_ref[g * units + slot]] * BLK
         limit = live - member * count
@@ -212,11 +253,12 @@
         pl.when(i < units)(lambda: forward(i))
         pl.when(i + AHEAD < units)(lambda: later(i + AHEAD))
         pl.when(i == 1)(panel.wait)
-        pl.when((i >= 1) & (i < units + 1))(lambda: attend(i - 1))
-        pl.when(i >= 2)(lambda: give_back(i - 2))
-        return carry
-
-    lax.fori_loop(0, units + 2, stage, 0)
+        pl.when((i >= 1) & (i < units + 1) & (lax.rem(i, 2) == 1))(lambda: swap(i - 1))
+        pl.when((i >= 2) & (i < units + 2))(lambda: attend(i - 2))
+        pl.when(i >= 3)(lambda: give_back(i - 3))
+        return carry
+
+    lax.fori_loop(0, units + 3, stage, 0)
 
     def arrived(u, carry):
         for dz in range(lines):
@@ -238,17 +280,35 @@
     def drain(u, carry):
         t = u // cap
         for dz in range(lines):
-            def both():
+            line = add(z, lines - dz, lines)
+
+            def sent():
                 ready(qown.at[u], s1.at[u, dz])
+
+            def passed():
+                for dx in range(1, rows):
+                    ready(qbuf.at[u, x, line], s2.at[u, dx, dz])
+
+            def returned():
                 ready(ssum.at[u, add(z, dz, lines)], s4.at[u, dz])
 
+            if dz % 2:
+                pl.when(direct(u))(sent)
+                pl.when(direct(u))(passed)
+            else:
+                if dz:
+                    sent()
+                else:
+                    pl.when(t > 0)(sent)
+                passed()
+                pl.when(jnp.logical_not(direct(u)))(
+                    lambda: ready(qbuf.at[u, :, line], s5.at[u, dz])
+                )
             if dz:
-                both()
-            else:
-                pl.when(t > 0)(both)
-        for dx in range(1, rows):
-            for dz in range(lines):
-                ready(qbuf.at[u, x, add(z, lines - dz, lines)], s2.at[u, dx, dz])
+                returned()
+            else:
+                pl.when(t > 0)(returned)
+        for dx in range(1, rows):
             ready(pbuf.at[u, add(x, dx, rows)], s3.at[u, dx])
         return carry
 
@@ -287,6 +347,8 @@
             sem((units, rows)),
             sem((units, lines)),
             sem((units, lines)),
+            sem((units, lines)),
+            sem((units, lines)),
         ],
         compiler_params=pltpu.CompilerParams(
             collective_id=0, has_side_effects=True, vmem_limit_bytes=56 * 1024 * 1024

time: 237 us -> 228 us (0.962)
  Pallas kernels: 216 us -> 207 us
    pallas_call x1, Pallas kernels: 216 us -> 207 us  [exchange(): pl.pallas_call(functools.partial(kernel, (groups, lines, rows, cap)), out...]
where the time goes in v5:
time: 228 us
  Pallas kernels  207 us (91%)
  other arithmetic  9.41 us (4%)
  matrix products  6.23 us (3%)
  local copies, waits for them, and re-layouts  4.85 us (2%)
    pallas_call x1, Pallas kernels, exchange(): pl.pallas_call(functools.partial(kernel, (groups, lines, rows, cap)), out...  207 us
    dot_general x1, matrix products, on_device(): jnp.dot(normed, w_uq, preferred_element_type=jnp.float32)  4.97 us

profile of v5, /device:TPU:25, one launch (start us, length us, event | category | flops | bytes accessed | tf_op | source)
XLA Modules:
  0.0 227.7 jit_solution(7311944605011589171)
XLA Ops:
  0.0 0.0 copy-start
  0.0 0.0 copy-start.1
  0.0 1.0 fusion.5
  1.0 0.2 convert_reduce_fusion
  1.3 0.6 select_reduce_fusion.1.pos_ref
  1.9 0.6 select_reduce_fusion.slot_ref
  2.5 1.3 fusion.6.unit_ref
  3.8 2.1 bitcast_reduce_fusion
  6.0 2.3 %fusion.3 = f32[8,64]{1,0:T(8,128)S(1)} fusion(f32[8,64]{1,0:T(8,128)S(1)} %broadcast_multiply_fusion, bf16[64,8,1024]{2,1,0:T(8,128)(2,1)} %param.7), kind=kLoop, calls=%fused_computation.8 | loop fusion | flops 2096640 | bytes 1052672 | tf_op jit(solution)/shard_map/reduce_sum | solution.py:18
  8.3 0.0 copy-done.1
  8.3 0.6 fusion.4
  8.9 5.0 %divide_multiply_fusion = f32[512,2048]{1,0:T(8,128)S(1)} fusion(bf16[512,1024]{1,0:T(8,128)(2,1)S(1)} %bitcast.31, bf16[1024,2048]{1,0:T(8,128)(2,1)} %param.12), kind=kOutput, calls=%fused_computation | convolution fusion | flops 2151677952 | bytes 9437184 | tf_op jit(solution)/shard_map/dot_general | solution.py:375
  13.9 1.1 slice.12
  15.1 207.1 %shard_map.73 = f32[8,64,1024]{2,1,0:T(8,128)} custom-call(s32[8]{0:T(128)} %select_reduce_fusion.1.pos_ref, s32[32]{0:T(128)} %fusion.6.unit_ref, s32[8]{0:T(128)} %select_reduce_fusion.slot_ref, s32[32]{0:T(128)} %cache_ref.1, s32[32]{0:T(128)} %blocks_ref.1, bf16[8,64,1024]{2,1,0:T(8,128)(2,1)} %bitcast.30, bf16[8,256,2048]{2,1,0:T(8,128)(2,1)} %kv_hbm.1), custom_call_target="tpu_custom_call" | custom-call | flops 4294967296 | bytes 8388608 | tf_op jit(solution)/shard_map/pallas_call | solution.py:328
  222.1 0.0 copy-start.2
  222.2 0.1 slice.10
  222.3 1.4 copy-done.2
  223.7 0.5 multiply_convert_fusion
  224.2 0.6 copy.12
  224.8 0.0 copy-done
  224.8 1.3 fusion
  226.1 1.5 copy.18
  (6 shorter events, 0.1 us)
Async XLA Ops:
  0.0 224.8 %copy-start = (bf16[1024,1024]{1,0:T(8,128)(2,1)S(1)}, bf16[1024,1024]{1,0:T(8,128)(2,1)}, u32[]{:S(2)}) copy-start(bf16[1024,1024]{1,0:T(8,128)(2,1)} %param.13) | copy-start | bytes 6291460
  0.0 8.3 %copy-start.1 = (bf16[64,8,1024]{2,1,0:T(8,128)(2,1)S(1)}, bf16[64,8,1024]{2,1,0:T(8,128)(2,1)}, u32[]{:S(2)}) copy-start(bf16[64,8,1024]{2,1,0:T(8,128)(2,1)} %param.7) | copy-start | bytes 3145732
  222.1 1.6 copy-start.2

commit v6 on v5

--- a/solution.py
+++ b/solution.py
@@ -10,7 +10,7 @@
 HEADS = 8
 BLK = 128
 LINE = 4
-AHEAD = 2
+AHEAD = 3
 
 
 def layer_norm(values):
@@ -253,8 +253,8 @@
         pl.when(i < units)(lambda: forward(i))
         pl.when(i + AHEAD < units)(lambda: later(i + AHEAD))
         pl.when(i == 1)(panel.wait)
+        pl.when((i >= 2) & (i < units + 2))(lambda: attend(i - 2))
         pl.when((i >= 1) & (i < units + 1) & (lax.rem(i, 2) == 1))(lambda: swap(i - 1))
-        pl.when((i >= 2) & (i < units + 2))(lambda: attend(i - 2))
         pl.when(i >= 3)(lambda: give_back(i - 3))
         return carry
 

time: 228 us -> 234 us (1.026)
  Pallas kernels: 207 us -> 213 us
    pallas_call x1, Pallas kernels: 207 us -> 213 us  [exchange(): pl.pallas_call(functools.partial(kernel, (groups, lines, rows, cap)), out...]
where the time goes in v6:
time: 234 us; the launch traced here: 233 us
  Pallas kernels  213 us (91%)
  other arithmetic  9.41 us (4%)
  matrix products  6.23 us (3%)
  local copies, waits for them, and re-layouts  4.85 us (2%)
    pallas_call x1, Pallas kernels, exchange(): pl.pallas_call(functools.partial(kernel, (groups, lines, rows, cap)), out...  213 us
    dot_general x1, matrix products, on_device(): jnp.dot(normed, w_uq, preferred_element_type=jnp.float32)  4.97 us

profile of v6, /device:TPU:25, one launch (start us, length us, event | category | flops | bytes accessed | tf_op | source)
XLA Modules:
  0.0 233.2 jit_solution(10296543517652303231)
XLA Ops:
  0.0 0.0 copy-start
  0.0 0.0 copy-start.1
  0.0 1.0 fusion.5
  1.0 0.2 convert_reduce_fusion
  1.3 0.6 select_reduce_fusion.1.pos_ref
  1.9 0.6 select_reduce_fusion.slot_ref
  2.5 1.3 fusion.6.unit_ref
  3.8 2.1 bitcast_reduce_fusion
  6.0 2.3 %fusion.3 = f32[8,64]{1,0:T(8,128)S(1)} fusion(f32[8,64]{1,0:T(8,128)S(1)} %broadcast_multiply_fusion, bf16[64,8,1024]{2,1,0:T(8,128)(2,1)} %param.7), kind=kLoop, calls=%fused_computation.8 | loop fusion | flops 2096640 | bytes 1052672 | tf_op jit(solution)/shard_map/reduce_sum | solution.py:18
  8.3 0.0 copy-done.1
  8.3 0.6 fusion.4
  8.9 5.0 %divide_multiply_fusion = f32[512,2048]{1,0:T(8,128)S(1)} fusion(bf16[512,1024]{1,0:T(8,128)(2,1)S(1)} %bitcast.31, bf16[1024,2048]{1,0:T(8,128)(2,1)} %param.12), kind=kOutput, calls=%fused_computation | convolution fusion | flops 2151677952 | bytes 9437184 | tf_op jit(solution)/shard_map/dot_general | solution.py:375
  13.9 1.1 slice.12
  15.1 212.6 %shard_map.73 = f32[8,64,1024]{2,1,0:T(8,128)} custom-call(s32[8]{0:T(128)} %select_reduce_fusion.1.pos_ref, s32[32]{0:T(128)} %fusion.6.unit_ref, s32[8]{0:T(128)} %select_reduce_fusion.slot_ref, s32[32]{0:T(128)} %cache_ref.1, s32[32]{0:T(128)} %blocks_ref.1, bf16[8,64,1024]{2,1,0:T(8,128)(2,1)} %bitcast.30, bf16[8,256,2048]{2,1,0:T(8,128)(2,1)} %kv_hbm.1), custom_call_target="tpu_custom_call" | custom-call | flops 4294967296 | bytes 8388608 | tf_op jit(solution)/shard_map/pallas_call | solution.py:328
  227.7 0.0 copy-start.2
  227.7 0.1 slice.10
  227.9 1.4 copy-done.2
  229.3 0.5 multiply_convert_fusion
  229.8 0.6 copy.12
  230.4 0.0 copy-done
  230.4 1.3 fusion
  231.7 1.5 copy.18
  (6 shorter events, 0.1 us)
Async XLA Ops:
  0.0 230.4 %copy-start = (bf16[1024,1024]{1,0:T(8,128)(2,1)S(1)}, bf16[1024,1024]{1,0:T(8,128)(2,1)}, u32[]{:S(2)}) copy-start(bf16[1024,1024]{1,0:T(8,128)(2,1)} %param.13) | copy-start | bytes 6291460
  0.0 8.3 %copy-start.1 = (bf16[64,8,1024]{2,1,0:T(8,128)(2,1)S(1)}, bf16[64,8,1024]{2,1,0:T(8,128)(2,1)}, u32[]{:S(2)}) copy-start(bf16[64,8,1024]{2,1,0:T(8,128)(2,1)} %param.7) | copy-start | bytes 3145732
  227.7 1.6 copy-start.2
